TPU v7x, 256 devices: a whole 4x4x8 slice. The times are simulated.
256 devices in a mesh: island: 32 (over y, z_hi, x), fsdp: 8 (over z_lo, core).
Axes of the slice: x: 4, y: 4, z: 8 (z_hi: 2, z_lo: 4; z = z_hi * 4 + z_lo), core: 2. Of those that a mesh axis runs over, the one named last changes fastest.
Arguments:
- tokens: bfloat16 [32, 2048, 12288], P('island', 'fsdp'), may hold values from -6 to 6
- targets: bfloat16 [32, 2048, 256], P('island', 'fsdp'), may hold values from -6 to 6
- loss_mask: int32 [32, 2048], P('island', 'fsdp'), may hold values 0 or 1
- norm_gain: float32 [12288], replicated, may hold values from 0.5 to 1.5
- params: float32 [32, 12288, 256], P('island', 'fsdp'), may hold values from -0.0546875 to 0.0546875
- moment_one: float32 [32, 12288, 256], P('island', 'fsdp'), may hold values from -0.12 to 0.12
- moment_two: float32 [32, 12288, 256], P('island', 'fsdp'), may hold values from 0.0001 to 0.002
- outer_delta: float32 [32, 12288, 128], P('island', 'fsdp'), may hold values from -6 to 6
- outer_momentum: float32 [12288, 128], P('fsdp'), may hold values from -6 to 6
Outputs:
- params_new: float32 [32, 12288, 256], P('island', 'fsdp')
- momentum_new: float32 [12288, 128], P('fsdp')
- outer_update: float32 [12288, 128], P('fsdp')
All inputs are finite; a program needn't handle non-finite values. No bound on the sum of `loss_mask` on one device may be relied on, other than what follows from the above.
Results may differ from a plain program's by a relative error of at most 0.0025.
Values may be sent and summed in bfloat16 or wider, within the bound.
No kernel may reach another device: no remote copies, remote signals or barrier semaphores. Data moves between devices by JAX's collectives and lax.ppermute only.
A program may use at most 128 MiB of HBM per device.

v0:
```python
import jax
import jax.numpy as jnp
from jax import lax
from jax.sharding import PartitionSpec as P

ADAM_BETA_ONE = 0.9
ADAM_BETA_TWO = 0.95
ADAM_EPSILON = 1e-08
INNER_RATE = 0.005
WEIGHT_DECAY = 0.1
NORM_EPSILON = 1e-05
OUTER_RATE = 0.7
OUTER_MOMENTUM = 0.9
STEP_BASE = 1000


def adam_update(weights, first_moment, second_moment, gradient, count):
    first_moment = ADAM_BETA_ONE * first_moment + (1.0 - ADAM_BETA_ONE) * gradient
    second_moment = ADAM_BETA_TWO * second_moment + (1.0 - ADAM_BETA_TWO) * gradient * gradient
    first_hat = first_moment / (1.0 - ADAM_BETA_ONE**count)
    second_hat = second_moment / (1.0 - ADAM_BETA_TWO**count)
    weights = weights - INNER_RATE * (
        first_hat / (jnp.sqrt(second_hat) + ADAM_EPSILON) + WEIGHT_DECAY * weights
    )
    return (weights, first_moment, second_moment)


def per_device(
    tokens,
    targets,
    loss_mask,
    norm_gain,
    params,
    moment_one,
    moment_two,
    outer_delta,
    outer_momentum,
):
    fsdp_count = lax.axis_size("fsdp")
    token_island = tokens.shape[1] * fsdp_count
    weights = params[0]
    first_moment = moment_one[0]
    second_moment = moment_two[0]
    inputs_f = tokens[0].astype(jnp.float32)
    row_scale = lax.rsqrt(jnp.mean(inputs_f * inputs_f, axis=1) + NORM_EPSILON)
    scaled = (inputs_f * norm_gain).astype(jnp.bfloat16)
    keep_rows = loss_mask[0].astype(jnp.float32)
    goal_rows = targets[0].astype(jnp.float32)
    for inner_step in range(2):
        weights_bf = weights.astype(jnp.bfloat16)
        empty_rows = jnp.zeros((scaled.shape[0], weights_bf.shape[1]), jnp.float32)
        shard_rows = lax.all_gather(weights_bf, "fsdp", axis=0, tiled=True)
        columns = lax.slice_in_dim(scaled, 0, shard_rows.shape[0], axis=1)
        projected = empty_rows + jnp.dot(columns, shard_rows, preferred_element_type=jnp.float32)
        value_rows = row_scale[:, None] * projected
        residual_rows = (
            row_scale[:, None] * keep_rows[:, None] * (value_rows - goal_rows) / token_island
        ).astype(jnp.bfloat16)
        gradient = lax.psum_scatter(
            lax.dot_general(
                scaled, residual_rows, (((0,), (0,)), ((), ())), preferred_element_type=jnp.float32
            ).astype(jnp.bfloat16),
            "fsdp",
            scatter_dimension=0,
            tiled=True,
        ).astype(jnp.float32)
        weights, first_moment, second_moment = adam_update(
            weights, first_moment, second_moment, gradient, float(STEP_BASE + inner_step + 1)
        )
    island_count = lax.axis_size("island")
    summed = lax.psum(outer_delta[0], "island")
    outer_mean = summed / island_count
    momentum_new = OUTER_MOMENTUM * outer_momentum + outer_mean
    outer_update = OUTER_RATE * (outer_mean + OUTER_MOMENTUM * momentum_new)
    momentum_new, outer_update = (momentum_new, outer_update)
    return (weights[None], momentum_new, outer_update)


def solution(mesh):
    return jax.shard_map(
        per_device,
        mesh=mesh,
        in_specs=(
            P("island", "fsdp", None),
            P("island", "fsdp", None),
            P("island", "fsdp"),
            P(),
            P("island", "fsdp", None),
            P("island", "fsdp", None),
            P("island", "fsdp", None),
            P("island", "fsdp", None),
            P("fsdp", None),
        ),
        out_specs=(P("island", "fsdp", None), P("fsdp", None), P("fsdp", None)),
        check_vma=False,
    )
```

profile of v0, /device:TPU:2, one launch (start us, length us, event | category | flops | bytes accessed | tf_op | source)
XLA Modules:
  0.0 686.9 jit_solution(9102844403319246760)
XLA Ops:
  8.0 0.0 copy-start.2
  8.0 0.0 all-gather.3.cloned.1.call-start
  8.1 2.4 bitcast_convert_fusion
  10.4 0.0 all-gather.3.cloned.1.call-update
  10.4 0.0 reduce-scatter.3.cloned.1.call-start
  10.5 0.0 copy-done.2
  10.5 0.0 copy-start.3
  10.5 0.0 copy-start.4
  10.5 4.2 fusion.1
  14.7 73.8 %all-gather.3.cloned.1.call-done = bf16[12288,256]{1,0:T(8,128)(2,1)} async-done(((bf16[1536,256]{1,0:T(8,128)(2,1)}), bf16[12288,256]{1,0:T(8,128)(2,1)}) %all-gather.3.cloned.1.call-update) | async-done | bytes 6291472 | tf_op jit(solution)/shard_map/all_gather | solution.py:52
  88.6 0.0 copy-done.3
  88.6 0.0 copy-done.4
  88.6 6.4 fusion.48
  95.0 7.5 %convolution_convert_fusion.1 = bf16[12288,256]{1,0:T(8,128)(2,1)} fusion(bf16[256,256]{1,0:T(8,128)(2,1)S(1)} %fusion.48, bf16[1,256,12288]{2,1,0:T(8,128)(2,1)} %param.9, f32[12288]{0:T(1024)S(1)} %copy-done.4), kind=kOutput, calls=%fused_computation.3 | convolution fusion | flops 1623195648 | bytes 12763136 | tf_op jit(solution)/shard_map/dot_general | solution.py:60
  102.5 0.0 copy-start
  102.5 0.0 reduce-scatter.3.cloned.1.call-update
  102.5 0.0 all-gather.5.cloned.1.call-start
  102.6 73.8 %reduce-scatter.3.cloned.1.call-done = bf16[1536,256]{1,0:T(8,128)(2,1)} async-done(((bf16[12288,256]{1,0:T(8,128)(2,1)}), bf16[1536,256]{1,0:T(8,128)(2,1)}) %reduce-scatter.3.cloned.1.call-update) | async-done | bytes 786448 | tf_op jit(solution)/shard_map/reduce_scatter | solution.py:59
  176.4 0.0 copy-done
  176.4 0.0 copy-done.1
  176.4 3.7 fusion.52
  180.1 0.0 all-gather.5.cloned.1.call-update
  180.1 0.0 all-reduce.2.cloned.1.call-start
  180.1 0.5 all-reduce.2.cloned.1.call-update
  180.7 0.2 reduce-scatter.5.cloned.1.call-start
  180.9 72.3 %all-gather.5.cloned.1.call-done = bf16[12288,256]{1,0:T(8,128)(2,1)} async-done(((bf16[1536,256]{1,0:T(8,128)(2,1)}), bf16[12288,256]{1,0:T(8,128)(2,1)}) %all-gather.5.cloned.1.call-update) | async-done | bytes 6291472 | tf_op jit(solution)/shard_map/all_gather | solution.py:52
  253.2 6.4 fusion.45
  259.6 7.5 %convolution_convert_fusion = bf16[12288,256]{1,0:T(8,128)(2,1)} fusion(bf16[256,256]{1,0:T(8,128)(2,1)S(1)} %fusion.45, bf16[1,256,12288]{2,1,0:T(8,128)(2,1)} %param.9, f32[12288]{0:T(1024)S(1)} %copy-done.4), kind=kOutput, calls=%fused_computation.2 | convolution fusion | flops 1623195648 | bytes 12763136 | tf_op jit(solution)/shard_map/dot_general | solution.py:60
  267.2 0.0 reduce-scatter.5.cloned.1.call-update
  267.2 404.6 %all-reduce.2.cloned.1.call-done = f32[1536,128]{1,0:T(8,128)} async-done(((f32[1536,128]{1,0:T(8,128)}), f32[1536,128]{1,0:T(8,128)}) %all-reduce.2.cloned.1.call-update) | async-done | bytes 786448 | tf_op jit(solution)/shard_map/psum | solution.py:71
  671.8 2.7 add_multiply_fusion
  674.5 5.3 fusion.14
  (4 shorter events, 0.0 us)
Async XLA Ops:
  8.0 2.5 copy-start.2
  8.0 80.6 %all-gather.3.cloned.1.call-start = ((), (), s32[]{:S(2)}) async-start(), calls=%async_computation.2 | async-start | bytes 7077888 | tf_op jit(solution)/shard_map/all_gather | solution.py:52
  10.4 165.9 %reduce-scatter.3.cloned.1.call-start = ((), (), s32[]{:S(2)}) async-start(), calls=%async_computation.3 | async-start | bytes 7077888 | tf_op jit(solution)/shard_map/reduce_scatter | solution.py:59
  10.5 78.0 %copy-start.3 = (bf16[1,256,256]{2,1,0:T(8,128)(2,1)S(1)}, bf16[1,256,256]{2,1,0:T(8,128)(2,1)}, u32[]{:S(2)}) copy-start(bf16[1,256,256]{2,1,0:T(8,128)(2,1)} %param.10) | copy-start | bytes 393220
  10.5 78.0 %copy-start.4 = (f32[12288]{0:T(1024)S(1)}, f32[12288]{0:T(1024)}, u32[]{:S(2)}) copy-start(f32[12288]{0:T(1024)} %param.12) | copy-start | bytes 147460
  102.5 73.9 %copy-start = (f32[1,1536,256]{2,1,0:T(8,128)S(1)}, f32[1,1536,256]{2,1,0:T(8,128)}, u32[]{:S(2)}) copy-start(f32[1,1536,256]{2,1,0:T(8,128)} %param.13) | copy-start | bytes 4718596
  102.5 73.9 %copy-start.1 = (f32[1,1536,256]{2,1,0:T(8,128)S(1)}, f32[1,1536,256]{2,1,0:T(8,128)}, u32[]{:S(2)}) copy-start(f32[1,1536,256]{2,1,0:T(8,128)} %param.15) | copy-start | bytes 4718596
  102.5 150.7 %all-gather.5.cloned.1.call-start = ((), (), s32[]{:S(2)}) async-start(), calls=%async_computation.4 | async-start | bytes 7077888 | tf_op jit(solution)/shard_map/all_gather | solution.py:52
  180.1 491.7 %all-reduce.2.cloned.1.call-start = ((), (), s32[]{:S(2)}) async-start(), calls=%async_computation.6 | async-start | bytes 1572864 | tf_op jit(solution)/shard_map/psum | solution.py:71
  180.7 493.8 %reduce-scatter.5.cloned.1.call-start = ((), (), s32[]{:S(2)}) async-start(), calls=%async_computation.5 | async-start | bytes 7077888 | tf_op jit(solution)/shard_map/reduce_scatter | solution.py:59
Sparse Core Ops, SparseCore 0:
  11.2 77.3 all-gather.2
  102.6 73.6 reduce-scatter.2
  180.2 72.9 all-gather.4
  267.3 77.1 reduce-scatter.4
Sparse Core Ops, SparseCore 1:
  183.2 488.6 all-reduce.1
where the time goes:
time: 687 us
  waiting for transfers between devices  625 us (91%)
  matrix products  27.9 us (4%)
  other arithmetic  18.2 us (3%)
  between operations  15.3 us (2%)
    psum x1, waiting for transfers between devices, per_device(): summed = lax.psum(outer_delta[0], 'island')  405 us
    all_gather x2, waiting for transfers between devices, per_device(): shard_rows = lax.all_gather(weights_bf, 'fsdp', axis=0, tiled=True)  146 us
    reduce_scatter x2, waiting for transfers between devices, per_device(): lax.psum_scatter(lax.dot_general(scaled, residual_rows, (((0,), (0,)), ((...  73.8 us
    dot_general x2, matrix products, per_device(): lax.dot_general(scaled, residual_rows, (((0,), (0,)), ((), ())), preferre...  15 us
  transfers between devices with their start and end apart: 5, of which 4 were waited for; matrix products, arithmetic and copies ran while one was open for 3% of the time, Pallas kernels for 0%

commit v1 on v0

--- a/solution.py
+++ b/solution.py
@@ -46,29 +46,41 @@
     scaled = (inputs_f * norm_gain).astype(jnp.bfloat16)
     keep_rows = loss_mask[0].astype(jnp.float32)
     goal_rows = targets[0].astype(jnp.float32)
+    halves = []
+    for h in range(2):
+        cols = slice(128 * h, 128 * h + 128)
+        halves.append([weights[:, cols], first_moment[:, cols], second_moment[:, cols], goal_rows[:, cols]])
     for inner_step in range(2):
-        weights_bf = weights.astype(jnp.bfloat16)
-        empty_rows = jnp.zeros((scaled.shape[0], weights_bf.shape[1]), jnp.float32)
-        shard_rows = lax.all_gather(weights_bf, "fsdp", axis=0, tiled=True)
-        columns = lax.slice_in_dim(scaled, 0, shard_rows.shape[0], axis=1)
-        projected = empty_rows + jnp.dot(columns, shard_rows, preferred_element_type=jnp.float32)
-        value_rows = row_scale[:, None] * projected
-        residual_rows = (
-            row_scale[:, None] * keep_rows[:, None] * (value_rows - goal_rows) / token_island
-        ).astype(jnp.bfloat16)
-        gradient = lax.psum_scatter(
-            lax.dot_general(
-                scaled, residual_rows, (((0,), (0,)), ((), ())), preferred_element_type=jnp.float32
-            ).astype(jnp.bfloat16),
-            "fsdp",
-            scatter_dimension=0,
-            tiled=True,
-        ).astype(jnp.float32)
-        weights, first_moment, second_moment = adam_update(
-            weights, first_moment, second_moment, gradient, float(STEP_BASE + inner_step + 1)
-        )
+        for h in range(2):
+            weights, first_moment, second_moment, goal = halves[h]
+            shard_rows = lax.all_gather(weights.astype(jnp.bfloat16), "fsdp", axis=0, tiled=True)
+            projected = jnp.dot(scaled, shard_rows, preferred_element_type=jnp.float32)
+            value_rows = row_scale[:, None] * projected
+            residual_rows = (
+                row_scale[:, None] * keep_rows[:, None] * (value_rows - goal) / token_island
+            ).astype(jnp.bfloat16)
+            gradient = lax.psum_scatter(
+                lax.dot_general(
+                    scaled, residual_rows, (((0,), (0,)), ((), ())), preferred_element_type=jnp.float32
+                ).astype(jnp.bfloat16),
+                "fsdp",
+                scatter_dimension=0,
+                tiled=True,
+            ).astype(jnp.float32)
+            halves[h][:3] = adam_update(
+                weights, first_moment, second_moment, gradient, float(STEP_BASE + inner_step + 1)
+            )
+    weights = jnp.concatenate([halves[0][0], halves[1][0]], axis=1)
     island_count = lax.axis_size("island")
-    summed = lax.psum(outer_delta[0], "island")
+    planes = [[(y * 2 + h) * 4 + x for y in range(4) for x in range(4)] for h in range(2)]
+    pieces = lax.all_to_all(
+        outer_delta[0], "island", 0, 0, axis_index_groups=planes, tiled=True
+    ).reshape(16, -1, outer_delta.shape[2])
+    part = jnp.sum(pieces, axis=0)
+    part = part + lax.ppermute(
+        part, "island", [((y * 2 + h) * 4 + x, (y * 2 + 1 - h) * 4 + x) for y in range(4) for h in range(2) for x in range(4)]
+    )
+    summed = lax.all_gather(part, "island", axis_index_groups=planes, axis=0, tiled=True)
     outer_mean = summed / island_count
     momentum_new = OUTER_MOMENTUM * outer_momentum + outer_mean
     outer_update = OUTER_RATE * (outer_mean + OUTER_MOMENTUM * momentum_new)

time: 687 us -> 403 us (0.59)
  waiting for transfers between devices: 625 us -> 274 us
  blocking collectives: 0 us -> 41.3 us
  matrix products: 27.9 us -> 45.5 us
    psum x1 -> x0, waiting for transfers between devices: 405 us -> none  [per_device(): summed = lax.psum(outer_delta[0], 'island')]
    reduce_scatter x2 -> x4, waiting for transfers between devices: 73.8 us -> 112 us  [per_device(): lax.psum_scatter(lax.dot_general(scaled, residual_rows, (((0,), (0,)), ((...]
    all_gather x0 -> x1, blocking collectives: none -> 23.1 us  [per_device(): lax.all_gather(part, 'island', axis_index_groups=planes, axis=0, tiled=True)]
    all_to_all x0 -> x1, blocking collectives: none -> 18.1 us  [per_device(): lax.all_to_all(outer_delta[0], 'island', 0, 0, axis_index_groups=planes,...]
    all_gather x2 -> x4, waiting for transfers between devices: 146 us -> 158 us  [per_device(): lax.all_gather(weights.astype(jnp.bfloat16), 'fsdp', axis=0, tiled=True)]
    dot_general x2 -> x4, matrix products: 12.8 us -> 22.2 us  [per_device(): projected = jnp.dot(scaled, shard_rows, preferred_element_type=jnp.float32)]
    dot_general x2 -> x4, matrix products: 15 us -> 23.3 us  [per_device(): lax.dot_general(scaled, residual_rows, (((0,), (0,)), ((), ())), preferre...]
  transfers between devices with their start and end apart: 5 -> 9, of which waited for: 4 -> 8; matrix products, arithmetic and copies ran while one was open for 3% -> 14% of each run, Pallas kernels for 0% -> 0%
where the time goes in v1:
time: 403 us; the launch traced here: 402 us
  waiting for transfers between devices  274 us (68%)
  matrix products  45.5 us (11%)
  blocking collectives  41.3 us (10%)
  other arithmetic  18.2 us (5%)
  between operations  14.2 us (4%)
  starting transfers between devices  6.34 us (2%)
    all_gather x4, waiting for transfers between devices, per_device(): lax.all_gather(weights.astype(jnp.bfloat16), 'fsdp', axis=0, tiled=True)  158 us
    reduce_scatter x4, waiting for transfers between devices, per_device(): lax.psum_scatter(lax.dot_general(scaled, residual_rows, (((0,), (0,)), ((...  112 us
    dot_general x4, matrix products, per_device(): lax.dot_general(scaled, residual_rows, (((0,), (0,)), ((), ())), preferre...  23.3 us
    all_gather x1, blocking collectives, per_device(): lax.all_gather(part, 'island', axis_index_groups=planes, axis=0, tiled=True)  23.1 us
    dot_general x4, matrix products, per_device(): projected = jnp.dot(scaled, shard_rows, preferred_element_type=jnp.float32)  22.2 us
    all_to_all x1, blocking collectives, per_device(): lax.all_to_all(outer_delta[0], 'island', 0, 0, axis_index_groups=planes,...  18.1 us
  transfers between devices with their start and end apart: 9, of which 8 were waited for; matrix products, arithmetic and copies ran while one was open for 14% of the time, Pallas kernels for 0%

profile of v1, /device:TPU:2, one launch (start us, length us, event | category | flops | bytes accessed | tf_op | source)
XLA Modules:
  0.0 402.1 jit_solution(1350848515283613460)
XLA Ops:
  7.2 2.4 fusion.49
  9.7 0.7 all-gather.5.cloned.1.call-update
  10.4 0.7 convert_element_type.76
  11.1 4.1 %fusion.1 = f32[256]{0:T(256)S(1)} fusion(bf16[1,256,12288]{2,1,0:T(8,128)(2,1)} %param.9), kind=kLoop, calls=%fused_computation.7 | loop fusion | flops 9436928 | bytes 6292480 | tf_op jit(solution)/shard_map/reduce_sum | solution.py:45
  15.3 43.0 %all-gather.9.cloned.1.call-done = bf16[12288,128]{1,0:T(8,128)(2,1)} async-done(((bf16[1536,128]{1,0:T(8,128)(2,1)}), bf16[12288,128]{1,0:T(8,128)(2,1)}) %all-gather.9.cloned.1.call-update) | async-done | bytes 3145744 | tf_op jit(solution)/shard_map/all_gather | solution.py:56
  58.2 5.7 %fusion.15 = bf16[256,128]{1,0:T(8,128)(2,1)S(1)} fusion(bf16[12288,128]{1,0:T(8,128)(2,1)} %all-gather.9.cloned.1.call-done, bf16[1,256,12288]{2,1,0:T(8,128)(2,1)} %param.9, f32[12288]{0:T(1024)S(1)} %copy-done.4, f32[256,256]{1,0:T(8,128)S(1)} %bitcast_convert_fusion, f32[256]{0:T(256)S(1)} %get-tuple-element.16, f32[256]{0:T(256)S(1)} %get-tuple-element.15), kind=kOutput, calls=%fused_computation.30 | convolution fusion | flops 814907392 | bytes 9684992 | tf_op jit(solution)/shard_map/dot_general | solution.py:57
  63.9 3.7 convolution_convert_fusion.1
  67.6 0.0 reduce-scatter.5.cloned.1.call-start
  67.7 36.7 %all-gather.5.cloned.1.call-done = bf16[12288,128]{1,0:T(8,128)(2,1)} async-done(((bf16[1536,128]{1,0:T(8,128)(2,1)}), bf16[12288,128]{1,0:T(8,128)(2,1)}) %all-gather.5.cloned.1.call-update) | async-done | bytes 3145744 | tf_op jit(solution)/shard_map/all_gather | solution.py:56
  104.3 5.5 %fusion.17 = bf16[256,128]{1,0:T(8,128)(2,1)S(1)} fusion(bf16[12288,128]{1,0:T(8,128)(2,1)} %all-gather.5.cloned.1.call-done, bf16[1,256,12288]{2,1,0:T(8,128)(2,1)} %param.9, f32[12288]{0:T(1024)S(1)} %copy-done.4, f32[256,256]{1,0:T(8,128)S(1)} %bitcast_convert_fusion, f32[256]{0:T(256)S(1)} %get-tuple-element.16, f32[256]{0:T(256)S(1)} %get-tuple-element.15), kind=kOutput, calls=%fused_computation.32 | convolution fusion | flops 814907392 | bytes 9684992 | tf_op jit(solution)/shard_map/dot_general | solution.py:57
  109.9 6.6 %convolution_convert_fusion.3 = bf16[12288,128]{1,0:T(8,128)(2,1)} fusion(bf16[256,128]{1,0:T(8,128)(2,1)S(1)} %fusion.17, bf16[1,256,12288]{2,1,0:T(8,128)(2,1)} %param.9, f32[12288]{0:T(1024)S(1)} %copy-done.4), kind=kOutput, calls=%fused_computation.5 | convolution fusion | flops 816316416 | bytes 9551872 | tf_op jit(solution)/shard_map/dot_general | solution.py:63
  116.6 34.8 %reduce-scatter.9.cloned.1.call-done = bf16[1536,128]{1,0:T(8,128)(2,1)} async-done(((bf16[12288,128]{1,0:T(8,128)(2,1)}), bf16[1536,128]{1,0:T(8,128)(2,1)}) %reduce-scatter.9.cloned.1.call-update) | async-done | bytes 393232 | tf_op jit(solution)/shard_map/reduce_scatter | solution.py:62
  151.4 47.9 %reduce-scatter.5.cloned.1.call-done = bf16[1536,128]{1,0:T(8,128)(2,1)} async-done(((bf16[12288,128]{1,0:T(8,128)(2,1)}), bf16[1536,128]{1,0:T(8,128)(2,1)}) %reduce-scatter.5.cloned.1.call-update) | async-done | bytes 393232 | tf_op jit(solution)/shard_map/reduce_scatter | solution.py:62
  199.3 3.8 fusion.47
  203.1 0.5 all-gather.7.cloned.1.call-update
  203.6 0.2 reduce-scatter.11.cloned.1.call-start
  203.9 44.0 %all-gather.11.cloned.1.call-done = bf16[12288,128]{1,0:T(8,128)(2,1)} async-done(((bf16[1536,128]{1,0:T(8,128)(2,1)}), bf16[12288,128]{1,0:T(8,128)(2,1)}) %all-gather.11.cloned.1.call-update) | async-done | bytes 3145744 | tf_op jit(solution)/shard_map/all_gather | solution.py:56
  247.9 5.5 %fusion.14 = bf16[256,128]{1,0:T(8,128)(2,1)S(1)} fusion(bf16[12288,128]{1,0:T(8,128)(2,1)} %all-gather.11.cloned.1.call-done, bf16[1,256,12288]{2,1,0:T(8,128)(2,1)} %param.9, f32[12288]{0:T(1024)S(1)} %copy-done.4, f32[256,256]{1,0:T(8,128)S(1)} %bitcast_convert_fusion, f32[256]{0:T(256)S(1)} %get-tuple-element.16, f32[256]{0:T(256)S(1)} %get-tuple-element.15), kind=kOutput, calls=%fused_computation.29 | convolution fusion | flops 814907392 | bytes 9684992 | tf_op jit(solution)/shard_map/dot_general | solution.py:57
  253.4 6.5 %convolution_convert_fusion = bf16[12288,128]{1,0:T(8,128)(2,1)} fusion(bf16[256,128]{1,0:T(8,128)(2,1)S(1)} %fusion.14, bf16[1,256,12288]{2,1,0:T(8,128)(2,1)} %param.9, f32[12288]{0:T(1024)S(1)} %copy-done.4), kind=kOutput, calls=%fused_computation.2 | convolution fusion | flops 816316416 | bytes 9551872 | tf_op jit(solution)/shard_map/dot_general | solution.py:63
  259.9 33.9 %all-gather.7.cloned.1.call-done = bf16[12288,128]{1,0:T(8,128)(2,1)} async-done(((bf16[1536,128]{1,0:T(8,128)(2,1)}), bf16[12288,128]{1,0:T(8,128)(2,1)}) %all-gather.7.cloned.1.call-update) | async-done | bytes 3145744 | tf_op jit(solution)/shard_map/all_gather | solution.py:56
  293.8 5.5 %fusion.16 = bf16[256,128]{1,0:T(8,128)(2,1)S(1)} fusion(bf16[12288,128]{1,0:T(8,128)(2,1)} %all-gather.7.cloned.1.call-done, bf16[1,256,12288]{2,1,0:T(8,128)(2,1)} %param.9, f32[12288]{0:T(1024)S(1)} %copy-done.4, f32[256,256]{1,0:T(8,128)S(1)} %bitcast_convert_fusion, f32[256]{0:T(256)S(1)} %get-tuple-element.16, f32[256]{0:T(256)S(1)} %get-tuple-element.15), kind=kOutput, calls=%fused_computation.31 | convolution fusion | flops 814907392 | bytes 9684992 | tf_op jit(solution)/shard_map/dot_general | solution.py:57
  299.3 6.5 %convolution_convert_fusion.2 = bf16[12288,128]{1,0:T(8,128)(2,1)} fusion(bf16[256,128]{1,0:T(8,128)(2,1)S(1)} %fusion.16, bf16[1,256,12288]{2,1,0:T(8,128)(2,1)} %param.9, f32[12288]{0:T(1024)S(1)} %copy-done.4), kind=kOutput, calls=%fused_computation.4 | convolution fusion | flops 816316416 | bytes 9551872 | tf_op jit(solution)/shard_map/dot_general | solution.py:63
  305.9 18.1 %all_to_all.9 = f32[16,96,128]{2,1,0:T(8,128)} all-to-all(f32[16,96,128]{2,1,0:T(8,128)} %bitcast.38), channel_id=1, replica_groups={{0,8,16,24,64,72,80,88,128,136,144,152,192,200,208,216},{32,40,48,56,96..., dimensions={0} | all-to-all | bytes 1572864 | tf_op jit(solution)/shard_map/all_to_all | solution.py:76
  324.0 1.8 reduce_sum.19
  325.8 5.8 %collective-permute-start = (f32[96,128]{1,0:T(8,128)}, f32[96,128]{1,0:T(8,128)S(1)}, u32[]{:S(2)}, u32[]{:S(2)}) collective-permute-start(f32[96,128]{1,0:T(8,128)} %reduce_sum.19), channel_id=1, source_target_pairs={{0,32},{8,40},{16,48},{24,56},{32,0},{40,8},{48,16},{56,24},{64,96... | collective-permute-start | bytes 147464 | tf_op jit(solution)/shard_map/ppermute | solution.py:80
  331.6 3.6 collective-permute-done
  335.2 0.8 add.96
  336.0 23.1 %all_gather.19 = f32[1536,128]{1,0:T(8,128)S(1)} all-gather(f32[96,128]{1,0:T(8,128)S(1)} %add.96), channel_id=1, replica_groups={{0,8,16,24,64,72,80,88,128,136,144,152,192,200,208,216},{32,40,48,56,96..., dimensions={0}, use_global_device_ids=true | all-gather | bytes 835584 | tf_op jit(solution)/shard_map/all_gather | solution.py:83
  359.2 2.5 add_multiply_fusion
  361.7 29.1 %reduce-scatter.7.cloned.1.call-done = bf16[1536,128]{1,0:T(8,128)(2,1)} async-done(((bf16[12288,128]{1,0:T(8,128)(2,1)}), bf16[1536,128]{1,0:T(8,128)(2,1)}) %reduce-scatter.7.cloned.1.call-update) | async-done | bytes 393232 | tf_op jit(solution)/shard_map/reduce_scatter | solution.py:62
  390.7 3.2 fusion.31
  394.0 1.2 maximum_bitcast_fusion
  (30 shorter events, 0.4 us)
Async XLA Ops:
  7.2 8.1 %copy-start.3 = (bf16[1,256,256]{2,1,0:T(8,128)(2,1)S(1)}, bf16[1,256,256]{2,1,0:T(8,128)(2,1)}, u32[]{:S(2)}) copy-start(bf16[1,256,256]{2,1,0:T(8,128)(2,1)} %param.10) | copy-start | bytes 393220
  7.2 51.1 %copy-start.4 = (f32[12288]{0:T(1024)S(1)}, f32[12288]{0:T(1024)}, u32[]{:S(2)}) copy-start(f32[12288]{0:T(1024)} %param.12) | copy-start | bytes 147460
  7.2 51.1 %all-gather.9.cloned.1.call-start = ((), (), s32[]{:S(2)}) async-start(), calls=%async_computation.9 | async-start | bytes 3538944 | tf_op jit(solution)/shard_map/all_gather | solution.py:56
  9.6 94.7 %all-gather.5.cloned.1.call-start = ((), (), s32[]{:S(2)}) async-start(), calls=%async_computation.5 | async-start | bytes 3538944 | tf_op jit(solution)/shard_map/all_gather | solution.py:56
  10.4 141.0 %reduce-scatter.9.cloned.1.call-start = ((), (), s32[]{:S(2)}) async-start(), calls=%async_computation.10 | async-start | bytes 3538944 | tf_op jit(solution)/shard_map/reduce_scatter | solution.py:62
  15.2 48.7 %slice-start = ((s8[6291456]{0:T(1024)(128)(4,1)}), s8[2097152]{0:T(1024)(128)(4,1)S(1)}, s32[]{:S(2)}) async-start(s8[6291456]{0:T(1024)(128)(4,1)} %bitcast.30), calls=%async_computation.13 | async-start | bytes 4194304
  58.2 5.7 %slice-start.1 = ((s8[6291456]{0:T(1024)(128)(4,1)}), s8[4194304]{0:T(1024)(128)(4,1)S(1)}, s32[]{:S(2)}) async-start(s8[6291456]{0:T(1024)(128)(4,1)} %bitcast.30), calls=%async_computation.14 | async-start | bytes 8388608
  67.6 131.6 %reduce-scatter.5.cloned.1.call-start = ((), (), s32[]{:S(2)}) async-start(), calls=%async_computation.6 | async-start | bytes 3538944 | tf_op jit(solution)/shard_map/reduce_scatter | solution.py:62
  109.9 89.4 %copy-start = (f32[1,1536,256]{2,1,0:T(8,128)S(1)}, f32[1,1536,256]{2,1,0:T(8,128)}, u32[]{:S(2)}) copy-start(f32[1,1536,256]{2,1,0:T(8,128)} %param.15) | copy-start | bytes 4718596
  109.9 89.4 %copy-start.1 = (f32[1,1536,256]{2,1,0:T(8,128)S(1)}, f32[1,1536,256]{2,1,0:T(8,128)}, u32[]{:S(2)}) copy-start(f32[1,1536,256]{2,1,0:T(8,128)} %param.14) | copy-start | bytes 4718596
  116.6 131.3 %all-gather.11.cloned.1.call-start = ((), (), s32[]{:S(2)}) async-start(), calls=%async_computation.11 | async-start | bytes 3538944 | tf_op jit(solution)/shard_map/all_gather | solution.py:56
  203.0 90.8 %all-gather.7.cloned.1.call-start = ((), (), s32[]{:S(2)}) async-start(), calls=%async_computation.7 | async-start | bytes 3538944 | tf_op jit(solution)/shard_map/all_gather | solution.py:56
  203.6 158.0 %reduce-scatter.11.cloned.1.call-start = ((), (), s32[]{:S(2)}) async-start(), calls=%async_computation.12 | async-start | bytes 3538944 | tf_op jit(solution)/shard_map/reduce_scatter | solution.py:62
  259.9 130.9 %reduce-scatter.7.cloned.1.call-start = ((), (), s32[]{:S(2)}) async-start(), calls=%async_computation.8 | async-start | bytes 3538944 | tf_op jit(solution)/shard_map/reduce_scatter | solution.py:62
  305.8 84.9 %copy-start.2 = (bf16[1536,128]{1,0:T(8,128)(2,1)S(1)}, bf16[1536,128]{1,0:T(8,128)(2,1)}, u32[]{:S(2)}) copy-start(bf16[1536,128]{1,0:T(8,128)(2,1)} %reduce-scatter.9.cloned.1.call-done) | copy-start | bytes 1179652
  325.8 9.4 %collective-permute-start = (f32[96,128]{1,0:T(8,128)}, f32[96,128]{1,0:T(8,128)S(1)}, u32[]{:S(2)}, u32[]{:S(2)}) collective-permute-start(f32[96,128]{1,0:T(8,128)} %reduce_sum.19), channel_id=1, source_target_pairs={{0,32},{8,40},{16,48},{24,56},{32,0},{40,8},{48,16},{56,24},{64,96... | collective-permute-start | bytes 147464 | tf_op jit(solution)/shard_map/ppermute | solution.py:80
Sparse Core Ops, SparseCore 0:
  10.4 47.8 all-gather.8
  60.6 43.6 all-gather.4
  106.9 44.4 reduce-scatter.8
  153.8 45.3 reduce-scatter.4
  203.2 44.6 all-gather.10
  250.1 43.6 all-gather.6
  296.4 46.5 reduce-scatter.10
  345.5 45.1 reduce-scatter.6
